TPU v7x, 128 devices: a whole 4x4x4 slice. The times are simulated.
128 devices in a mesh: dp: 16 (over x, y_lo, core), row: 4 (over z), col: 2 (over y_hi).
Axes of the slice: x: 4, y: 4 (y_hi: 2, y_lo: 2; y = y_hi * 2 + y_lo), z: 4, core: 2. Of those that a mesh axis runs over, the one named last changes fastest.
Arguments:
- activations: bfloat16 [16384, 896], P('dp', 'row'), may hold values from -6 to 6
- starts: int32 [16384], P('dp'), may hold values from 0 to 16383, as said below
- first_gain: float32 [896], P('row'), may hold values from 0.5 to 1.5
- project_weight: bfloat16 [896, 1152], P('row', 'col'), may hold values from -0.1875 to 0.1875
- project_bias: float32 [1152], P('col'), may hold values from -3 to 3
- output_weight: bfloat16 [896, 896], P('col', 'row'), may hold values from -0.75 to 0.75
- second_gain: float32 [896], P('row'), may hold values from 0.5 to 1.5
- gate_weight: bfloat16 [896, 4864], P('row', 'col'), may hold values from -0.1875 to 0.1875
- up_weight: bfloat16 [896, 4864], P('row', 'col'), may hold values from -0.1875 to 0.1875
- down_weight: bfloat16 [4864, 896], P('col', 'row'), may hold values from -0.15625 to 0.15625
- cotangent: bfloat16 [16384, 896], P('dp', 'row'), may hold values from -6 to 6
Outputs:
- block_output: bfloat16 [16384, 896], P('dp', 'row')
- input_grad: float32 [16384, 896], P('dp', 'row')
- first_gain_grad: float32 [896], P('row')
- project_weight_grad: float32 [896, 1152], P('row', 'col')
- project_bias_grad: float32 [1152], P('col')
- output_weight_grad: float32 [896, 896], P('col', 'row')
- second_gain_grad: float32 [896], P('row')
- gate_weight_grad: float32 [896, 4864], P('row', 'col')
- up_weight_grad: float32 [896, 4864], P('row', 'col')
- down_weight_grad: float32 [4864, 896], P('col', 'row')
Inputs may be any that keep to these rules, and one draw needn't show every extreme that they name: starts never falls, starts[t] <= t, and starts[t] is t or starts[t - 1]; a sequence holds at most 1024 tokens, and one holds exactly 1024.
All inputs are finite; a program needn't handle non-finite values.
Results may differ from a plain program's by a relative error of at most 0.012.
Values may be sent and summed in bfloat16 or wider, within the bound.
A program may use at most 192 MiB of HBM per device.

v0:
```python
import jax
import jax.numpy as jnp
from jax import lax
from jax.sharding import PartitionSpec as P

D = 896
HEADS = 14
GROUPS = 2
HEAD_DIM = 64
MAXLEN = 1024


EPS = 1e-06


def from_behind(block, axis, distance):
    devices = range(lax.axis_size(axis))
    route = [(i - distance, i) for i in devices if i - distance in devices]
    return lax.ppermute(block, axis, route)


def rotate(values, positions, sign):
    half = HEAD_DIM // 2
    freqs = 1000000.0 ** (-jnp.arange(half, dtype=jnp.float32) * 2.0 / HEAD_DIM)
    angle = positions.astype(jnp.float32)[:, None] * freqs[None, :]
    cosine = jnp.cos(angle)
    sine = sign * jnp.sin(angle)
    if values.ndim == 3:
        cosine = cosine[:, None, :]
        sine = sine[:, None, :]
    first = values[..., :half]
    second = values[..., half:]
    return jnp.concatenate(
        [first * cosine - second * sine, second * cosine + first * sine], axis=-1
    )


def row_total(values):
    return lax.psum(values, "row")


def column_sum(values):
    return lax.psum(values, "col")


def project_rows(normed, weights):
    return lax.psum_scatter(
        jnp.concatenate(
            [jnp.dot(normed, weight, preferred_element_type=jnp.float32) for weight in weights],
            axis=1,
        ),
        "row",
        scatter_dimension=0,
        tiled=True,
    )


def return_rows(grads, weight):
    return lax.psum_scatter(
        lax.dot_general(
            grads, weight, (((1,), (1,)), ((), ())), preferred_element_type=jnp.float32
        ),
        "row",
        scatter_dimension=0,
        tiled=True,
    )


def spread_rows(values, weight):
    piece = lax.all_gather(values, "row", axis=0, tiled=True)
    return (jnp.dot(piece, weight, preferred_element_type=jnp.float32), piece)


def weight_grad(kept, grads):
    return lax.dot_general(
        kept, grads, (((0,), (0,)), ((), ())), preferred_element_type=jnp.float32
    )


def fold_rows(grads, normed, weights):
    piece = lax.all_gather(grads, "row", axis=0, tiled=True)
    totals = tuple(
        (jnp.zeros((normed.shape[1], weight.shape[1]), jnp.float32) for weight in weights)
    )
    count = piece.shape[0]
    offset = 0
    contrib = jnp.zeros((count, normed.shape[1]), jnp.float32)
    updated = []
    for weight, total in zip(weights, totals):
        portion = piece[:, offset : offset + weight.shape[1]]
        offset = offset + weight.shape[1]
        contrib = contrib + lax.dot_general(
            portion, weight, (((1,), (1,)), ((), ())), preferred_element_type=jnp.float32
        )
        updated.append(
            lax.dot_general(
                normed, portion, (((0,), (0,)), ((), ())), preferred_element_type=jnp.float32
            )
        )
    column_total = jnp.sum(piece.astype(jnp.float32), axis=0)
    return (contrib, tuple(updated), column_total)


def masked_scores(queries, key_part, allowed):
    scores = jnp.einsum(
        "qmd,kd->mqk", queries, key_part, preferred_element_type=jnp.float32
    ) * HEAD_DIM ** (-0.5)
    return jnp.where(allowed[None], scores, -1e30)


def attend_forward(queries, pairs, allowed):
    scores = masked_scores(queries, pairs[:, :HEAD_DIM], allowed)
    peak = jnp.max(scores, axis=-1, keepdims=True)
    powered = jnp.exp(scores - peak)
    denominator = jnp.sum(powered, axis=-1, keepdims=True)
    probs = (powered / denominator).astype(jnp.bfloat16)
    mixed = jnp.einsum(
        "mqk,kd->qmd", probs, pairs[:, HEAD_DIM:], preferred_element_type=jnp.float32
    )
    return (mixed, peak + jnp.log(denominator))


def attend_backward(queries, pairs, allowed, log_total, grad_mixed):
    key_part = pairs[:, :HEAD_DIM]
    value_part = pairs[:, HEAD_DIM:]
    scores = masked_scores(queries, key_part, allowed)
    probs = jnp.exp(scores - log_total)
    probs_low = probs.astype(jnp.bfloat16)
    grad_values = jnp.einsum(
        "mqk,qmd->kd", probs_low, grad_mixed, preferred_element_type=jnp.float32
    )
    grad_probs = jnp.einsum(
        "qmd,kd->mqk", grad_mixed, value_part, preferred_element_type=jnp.float32
    )
    inner_sum = jnp.sum(probs * grad_probs, axis=-1, keepdims=True)
    grad_scores = (probs * (grad_probs - inner_sum)).astype(jnp.bfloat16)
    grad_queries = jnp.einsum(
        "mqk,kd->qmd", grad_scores, key_part, preferred_element_type=jnp.float32
    ) * HEAD_DIM ** (-0.5)
    grad_keys = jnp.einsum(
        "mqk,qmd->kd", grad_scores, queries, preferred_element_type=jnp.float32
    ) * HEAD_DIM ** (-0.5)
    return (grad_queries, jnp.concatenate([grad_keys, grad_values], axis=1))


def body(
    activations,
    starts,
    first_gain,
    project_weight,
    project_bias,
    output_weight,
    second_gain,
    gate_weight,
    up_weight,
    down_weight,
    cotangent,
):
    shard_rows = activations.shape[0]
    share = shard_rows // lax.axis_size("row")
    row_index = lax.axis_index("row")
    shard_index = lax.axis_index("dp")
    group_heads = HEADS // GROUPS
    query_width = group_heads * HEAD_DIM
    local_index = row_index * share + jnp.arange(share, dtype=jnp.int32)
    start_local = (
        lax.dynamic_slice_in_dim(starts, row_index * share, share, 0) - shard_index * shard_rows
    )
    positions = local_index - start_local
    key_local = jnp.arange(MAXLEN + shard_rows, dtype=jnp.int32) - MAXLEN
    allowed = (key_local[None, :] >= start_local[:, None]) & (
        key_local[None, :] <= local_index[:, None]
    )
    inputs = activations.astype(jnp.float32)
    first_rate = lax.rsqrt(row_total(jnp.sum(inputs * inputs, axis=1)) / D + EPS)
    normed_first = (inputs * first_rate[:, None] * first_gain).astype(jnp.bfloat16)
    projected = project_rows(normed_first, (project_weight,)) + project_bias
    queries = rotate(
        projected[:, :query_width].reshape(share, group_heads, HEAD_DIM), positions, 1.0
    ).astype(jnp.bfloat16)
    keys_new = rotate(projected[:, query_width : query_width + HEAD_DIM], positions, 1.0)
    pair_share = jnp.concatenate([keys_new, projected[:, query_width + HEAD_DIM :]], axis=1).astype(
        jnp.bfloat16
    )
    shard_pairs = lax.all_gather(pair_share, "row", axis=0, tiled=True)
    earlier = from_behind(shard_pairs, "dp", 1)
    pairs = jnp.concatenate([earlier, shard_pairs], axis=0)
    mixed, log_total = attend_forward(queries, pairs, allowed)
    attended = mixed.reshape(share, query_width).astype(jnp.bfloat16)
    attention_partial, attended_all = spread_rows(attended, output_weight)
    middle = inputs + column_sum(attention_partial)
    second_rate = lax.rsqrt(row_total(jnp.sum(middle * middle, axis=1)) / D + EPS)
    normed_second = (middle * second_rate[:, None] * second_gain).astype(jnp.bfloat16)
    gate_up = project_rows(normed_second, (gate_weight, up_weight))
    hidden_width = gate_weight.shape[1]
    gate_values = gate_up[:, :hidden_width]
    up_values = gate_up[:, hidden_width:]
    hidden = (jax.nn.silu(gate_values) * up_values).astype(jnp.bfloat16)
    hidden_partial, hidden_all = spread_rows(hidden, down_weight)
    block_output = (middle + column_sum(hidden_partial)).astype(jnp.bfloat16)
    grad_output = cotangent.astype(jnp.float32)
    grad_hidden = return_rows(cotangent, down_weight)
    down_grad = weight_grad(hidden_all, cotangent)
    sigma = jax.nn.sigmoid(gate_values)
    grad_gate = grad_hidden * up_values * sigma * (1.0 + gate_values * (1.0 - sigma))
    grad_up = grad_hidden * gate_values * sigma
    grad_gate_up = jnp.concatenate([grad_gate, grad_up], axis=1).astype(jnp.bfloat16)
    second_partial, hidden_grads, unused_total = fold_rows(
        grad_gate_up, normed_second, (gate_weight, up_weight)
    )
    gate_grad, up_grad = hidden_grads
    grad_second = column_sum(second_partial)
    weighted_second = grad_second * second_gain
    second_inner = row_total(jnp.sum(weighted_second * middle, axis=1))
    second_gain_grad = jnp.sum(grad_second * middle * second_rate[:, None], axis=0)
    grad_middle = (
        grad_output
        + second_rate[:, None] * weighted_second
        - middle * (second_rate**3 * second_inner / D)[:, None]
    )
    grad_branch = grad_middle.astype(jnp.bfloat16)
    grad_attended = (
        return_rows(grad_branch, output_weight)
        .astype(jnp.bfloat16)
        .reshape(share, group_heads, HEAD_DIM)
    )
    output_grad = weight_grad(attended_all, grad_branch)
    grad_queries, grad_pairs = attend_backward(queries, pairs, allowed, log_total, grad_attended)
    returned = from_behind(grad_pairs[:MAXLEN], "dp", -1)
    own_pairs = grad_pairs[MAXLEN:].at[shard_rows - MAXLEN :].add(returned)
    grad_pair = lax.psum_scatter(own_pairs, "row", scatter_dimension=0, tiled=True)
    grad_keys = rotate(grad_pair[:, :HEAD_DIM], positions, -1.0)
    grad_query_plain = rotate(grad_queries, positions, -1.0).reshape(share, query_width)
    grad_projected = jnp.concatenate(
        [grad_query_plain, grad_keys, grad_pair[:, HEAD_DIM:]], axis=1
    ).astype(jnp.bfloat16)
    first_partial, project_grads, bias_grad = fold_rows(
        grad_projected, normed_first, (project_weight,)
    )
    project_grad = project_grads[0]
    grad_first = column_sum(first_partial)
    weighted_first = grad_first * first_gain
    first_inner = row_total(jnp.sum(weighted_first * inputs, axis=1))
    first_gain_grad = jnp.sum(grad_first * inputs * first_rate[:, None], axis=0)
    input_grad = (
        grad_middle
        + first_rate[:, None] * weighted_first
        - inputs * (first_rate**3 * first_inner / D)[:, None]
    )
    (
        first_gain_grad,
        project_grad,
        bias_grad,
        output_grad,
        second_gain_grad,
        gate_grad,
        up_grad,
        down_grad,
    ) = lax.psum(
        (
            first_gain_grad,
            project_grad,
            bias_grad,
            output_grad,
            second_gain_grad,
            gate_grad,
            up_grad,
            down_grad,
        ),
        "dp",
    )
    return (
        block_output,
        input_grad,
        first_gain_grad,
        project_grad,
        bias_grad,
        output_grad,
        second_gain_grad,
        gate_grad,
        up_grad,
        down_grad,
    )


def solution(mesh):
    return jax.shard_map(
        body,
        mesh=mesh,
        in_specs=(
            P("dp", "row"),
            P("dp"),
            P("row"),
            P("row", "col"),
            P("col"),
            P("col", "row"),
            P("row"),
            P("row", "col"),
            P("row", "col"),
            P("col", "row"),
            P("dp", "row"),
        ),
        out_specs=(
            P("dp", "row"),
            P("dp", "row"),
            P("row"),
            P("row", "col"),
            P("col"),
            P("col", "row"),
            P("row"),
            P("row", "col"),
            P("row", "col"),
            P("col", "row"),
        ),
        check_vma=False,
    )
```

profile of v0, /device:TPU:1, one launch (start us, length us, event | category | flops | bytes accessed | tf_op | source)
XLA Modules:
  0.0 1050.0 jit_solution(14629089690623292735)
XLA Ops:
  8.5 10.6 %psum.112 = f32[1024]{0:T(1024)S(1)} all-reduce(f32[1024]{0:T(1024)S(1)} %fusion.26), channel_id=1, replica_groups=mesh['dp'=16,'row'=4,'col'=2] {'row'}, use_global_device_ids=true, to_apply=%region_1.0 | all-reduce | flops 1024 | bytes 8192 | tf_op jit(solution)/shard_map/psum | solution.py:39
  23.0 32.6 %reduce-scatter.6.cloned.1.call-done = f32[256,576]{0,1:T(8,128)} async-done(((f32[1024,576]{0,1:T(8,128)}), f32[256,576]{0,1:T(8,128)}) %reduce-scatter.6.cloned.1.call-update) | async-done | bytes 589840 | tf_op jit(solution)/shard_map/reduce_scatter | solution.py:47
  57.7 9.4 all_gather.15
  67.1 6.5 collective-permute-start
  77.0 6.5 fusion.65
  83.5 7.1 fusion.3
  90.6 6.7 fusion.25
  97.4 12.2 %all_gather.16 = bf16[1024,448]{0,1:T(8,128)(2,1)S(1)} all-gather(bf16[256,448]{0,1:T(8,128)(2,1)S(1)} %bitcast.69), channel_id=1, replica_groups=mesh['dp'=16,'row'=4,'col'=2] {'row'}, dimensions={0}, use_global_device_ids=true | all-gather | bytes 1146880 | tf_op jit(solution)/shard_map/all_gather | solution.py:70
  112.0 5.3 fusion.70
  117.4 43.0 %all-reduce.8.cloned.1.call-done = f32[1024,224]{0,1:T(8,128)} async-done(((f32[1024,224]{0,1:T(8,128)}), f32[1024,224]{0,1:T(8,128)}) %all-reduce.8.cloned.1.call-update) | async-done | bytes 917520 | tf_op jit(solution)/shard_map/psum | solution.py:43
  161.8 8.7 psum.114
  175.4 7.1 pad_maximum_fusion
  182.6 73.4 %reduce-scatter.10.cloned.1.call-done = f32[256,2432]{1,0:T(8,128)} async-done(((f32[1024,2432]{1,0:T(8,128)}), f32[256,2432]{1,0:T(8,128)}) %reduce-scatter.10.cloned.1.call-update) | async-done | bytes 2490384 | tf_op jit(solution)/shard_map/reduce_scatter | solution.py:59
  256.0 175.6 %reduce-scatter.8.cloned.1.call-done = f32[256,4864]{1,0:T(8,128)} async-done(((f32[1024,4864]{1,0:T(8,128)}), f32[256,4864]{1,0:T(8,128)}) %reduce-scatter.8.cloned.1.call-update) | async-done | bytes 4980752 | tf_op jit(solution)/shard_map/reduce_scatter | solution.py:47
  431.6 5.7 multiply_convert_fusion.1
  438.9 96.1 %all-gather.6.cloned.1.call-done = bf16[1024,4864]{1,0:T(8,128)(2,1)} async-done(((bf16[256,4864]{1,0:T(8,128)(2,1)}), bf16[1024,4864]{1,0:T(8,128)(2,1)}) %all-gather.6.cloned.1.call-update) | async-done | bytes 9961488 | tf_op jit(solution)/shard_map/all_gather | solution.py:81
  544.3 46.3 %all-reduce.10.cloned.1.call-done = f32[1024,224]{0,1:T(8,128)} async-done(((f32[1024,224]{0,1:T(8,128)}), f32[1024,224]{0,1:T(8,128)}) %all-reduce.10.cloned.1.call-update) | async-done | bytes 917520 | tf_op jit(solution)/shard_map/psum | solution.py:43
  592.1 8.7 psum.117
  604.2 26.8 %reduce-scatter.12.cloned.1.call-done = f32[256,448]{0,1:T(8,128)} async-done(((f32[1024,448]{0,1:T(8,128)}), f32[256,448]{0,1:T(8,128)}) %reduce-scatter.12.cloned.1.call-update) | async-done | bytes 458768 | tf_op jit(solution)/shard_map/reduce_scatter | solution.py:59
  632.1 11.8 %fusion = (f32[7,256]{1,0:T(8,128)S(1)}, f32[2048,256,7]{1,0,2:T(8,128)}) fusion(f32[7,256,2048]{1,2,0:T(8,128)} %get-tuple-element.65, f32[7,256]{1,0:T(8,128)S(1)} %log_add_fusion, bf16[256,7,64]{0,2,1:T(8,128)(2,1)S(1)} %bitcast.65, bf16[2048,128]{0,1:T(8,128)(2,1)} %copy-done.18), kind=kOutput, calls=%fused_computation.3 | convolution fusion | flops 480770304 | bytes 29865984 | tf_op jit(solution)/shard_map/qmd,kd->mqk/dot_general | solution.py:132
  648.4 7.2 fusion.2
  661.3 8.0 collective-permute-done.1
  675.7 14.3 %reduce-scatter.14.cloned.1.call-done = f32[256,128]{0,1:T(8,128)} async-done(((f32[1024,128]{0,1:T(8,128)}), f32[256,128]{0,1:T(8,128)}) %reduce-scatter.14.cloned.1.call-update) | async-done | bytes 131088 | tf_op jit(solution)/shard_map/reduce_scatter | solution.py:231
  692.6 56.0 %all-gather.4.cloned.1.call-done = bf16[1024,2432]{1,0:T(8,128)(2,1)} async-done(((bf16[256,2432]{1,0:T(8,128)(2,1)}), bf16[1024,2432]{1,0:T(8,128)(2,1)}) %all-gather.4.cloned.1.call-update) | async-done | bytes 4980752 | tf_op jit(solution)/shard_map/all_gather | solution.py:70
  748.7 5.0 fusion.69
  753.6 23.8 %all-gather.8.cloned.1.call-done = bf16[1024,576]{0,1:T(8,128)(2,1)} async-done(((bf16[256,576]{0,1:T(8,128)(2,1)}), bf16[1024,576]{0,1:T(8,128)(2,1)}) %all-gather.8.cloned.1.call-update) | async-done | bytes 1179664 | tf_op jit(solution)/shard_map/all_gather | solution.py:81
  780.6 5.3 fusion.72
  785.9 5.2 fusion.13
  798.3 49.3 %all-reduce.14.cloned.1.call-done = (f32[1024,224]{0,1:T(8,128)}, f32[1024,224]{0,1:T(8,128)}) async-done(((f32[1024,224]{0,1:T(8,128)}, f32[1024,224]{0,1:T(8,128)}), (f32[1024,224]{0,1:T(8,128)}, f32[1024,224]{0,1:T(8,128)})) %all-reduce.14.cloned.1.call-update) | async-done | bytes 1835024 | tf_op jit(solution)/shard_map/psum | solution.py:43
  849.1 28.7 %all-reduce = (f32[224]{0:T(256)}, f32[576]{0:T(1024)}, f32[224]{0:T(256)}) all-reduce(f32[224]{0:T(256)S(1)} %get-tuple-element.32, f32[576]{0:T(1024)S(1)} %convert_reduce_fusion, f32[224]{0:T(256)S(1)} %get-tuple-element.30), channel_id=1, replica_groups=mesh['dp'=16,'row'=4,'col'=2] {'dp'}, use_global_device_ids=true, to_apply=%region_21.22 | all-reduce | flops 1024 | bytes 8192 | tf_op jit(solution)/shard_map/psum | solution.py:259
  877.8 9.3 psum.119
  891.6 141.7 %all-reduce.12.cloned.1.call-done = (f32[224,576]{1,0:T(8,128)}, f32[448,224]{1,0:T(8,128)}, f32[224,2432]{1,0:T(8,128)}, f32[224,2432]{1,0:T(8,128)}, f32[2432,224]{0,1:T(8,128)}) async-done(((f32[224,576]{1,0:T(8,128)}, f32[448,224]{1,0:T(8,128)}, f32[224,2432]{1,0:T(8,128)}, f32[224,2432]{1,0:T(8,128)}, f32[2432,224]{0,1:T(8,128)}), (f32[224,576]{1,0:T(8,128)}, f32[448,224]{1,0:T(8,128)}, ...) | async-done | bytes 7454736 | tf_op jit(solution)/shard_map/psum | solution.py:259
  (171 shorter events, 81.3 us)
Async XLA Ops:
  7.2 166.7 %copy-start = (bf16[224,2432]{1,0:T(8,128)(2,1)S(1)}, bf16[224,2432]{1,0:T(8,128)(2,1)}, u32[]{:S(2)}) copy-start(bf16[224,2432]{1,0:T(8,128)(2,1)} %param.23) | copy-start | bytes 3268612
  7.2 48.5 %copy-start.33 = (f32[576]{0:T(1024)S(1)}, f32[576]{0:T(1024)}, u32[]{:S(2)}) copy-start(f32[576]{0:T(1024)} %param.19) | copy-start | bytes 6916
  7.2 48.5 %reduce-scatter.6.cloned.1.call-start = ((), (), s32[]{:S(2)}) async-start(), calls=%async_computation.5 | async-start | bytes 2949120 | tf_op jit(solution)/shard_map/reduce_scatter | solution.py:47
  22.2 138.2 %all-reduce.8.cloned.1.call-start = ((), (), s32[]{:S(2)}) async-start(), calls=%async_computation.6 | async-start | bytes 1835008 | tf_op jit(solution)/shard_map/psum | solution.py:43
  22.2 61.3 %copy-start.34 = (f32[32]{0:T(128)}, f32[32]{0:T(128)S(1)}, u32[]{:S(2)}) copy-start(f32[32]{0:T(128)S(1)} %multiply_power_fusion) | copy-start | bytes 388
  23.0 60.5 %copy-start.30 = (f32[256]{0:T(256)}, f32[256]{0:T(256)S(1)}, u32[]{:S(2)}) copy-start(f32[256]{0:T(256)S(1)} %get-tuple-element.46) | copy-start | bytes 3076
  57.7 25.8 %copy-start.26 = (f32[256,32]{0,1:T(8,128)}, f32[256,32]{0,1:T(8,128)S(1)}, u32[]{:S(2)}) copy-start(f32[256,32]{0,1:T(8,128)S(1)} %get-tuple-element.63) | copy-start | bytes 98308
  67.1 9.8 collective-permute-start
  90.6 19.9 %copy-start.23 = (bf16[448,224]{1,0:T(8,128)(2,1)S(1)}, bf16[448,224]{1,0:T(8,128)(2,1)}, u32[]{:S(2)}) copy-start(bf16[448,224]{1,0:T(8,128)(2,1)} %param.20) | copy-start | bytes 602116
  90.6 21.3 %copy-start.16 = (bf16[1024,224]{0,1:T(8,128)(2,1)S(1)}, bf16[1024,224]{0,1:T(8,128)(2,1)}, u32[]{:S(2)}) copy-start(bf16[1024,224]{0,1:T(8,128)(2,1)} %param.25) | copy-start | bytes 1376260
  90.6 21.3 %copy-start.21 = (bf16[2432,224]{0,1:T(8,128)(2,1)S(1)}, bf16[2432,224]{0,1:T(8,128)(2,1)}, u32[]{:S(2)}) copy-start(bf16[2432,224]{0,1:T(8,128)(2,1)} %param.24) | copy-start | bytes 3268612
  111.9 144.1 %reduce-scatter.10.cloned.1.call-start = ((), (), s32[]{:S(2)}) async-start(), calls=%async_computation.9 | async-start | bytes 12451840 | tf_op jit(solution)/shard_map/reduce_scatter | solution.py:59
  117.3 43.1 %copy-start.7 = (bf16[1024,224]{0,1:T(8,128)(2,1)S(1)}, bf16[1024,224]{0,1:T(8,128)(2,1)}, u32[]{:S(2)}) copy-start(bf16[1024,224]{0,1:T(8,128)(2,1)} %param.15) | copy-start | bytes 1376260
  117.3 53.1 %copy-start.29 = (f32[224]{0:T(256)S(1)}, f32[224]{0:T(256)}, u32[]{:S(2)}) copy-start(f32[224]{0:T(256)} %param.21) | copy-start | bytes 2692
  117.3 314.2 %reduce-scatter.8.cloned.1.call-start = ((), (), s32[]{:S(2)}) async-start(), calls=%async_computation.7 | async-start | bytes 24903680 | tf_op jit(solution)/shard_map/reduce_scatter | solution.py:47
  161.7 439.0 %copy-start.3 = (f32[1024,224]{0,1:T(8,128)}, f32[1024,224]{0,1:T(8,128)S(1)}, u32[]{:S(2)}) copy-start(f32[1024,224]{0,1:T(8,128)S(1)} %get-tuple-element.45) | copy-start | bytes 2752516
  182.5 352.6 %all-gather.6.cloned.1.call-start = ((), (), s32[]{:S(2)}) async-start(), calls=%async_computation.10 | async-start | bytes 12451840 | tf_op jit(solution)/shard_map/all_gather | solution.py:81
  438.9 151.7 %all-reduce.10.cloned.1.call-start = ((), (), s32[]{:S(2)}) async-start(), calls=%async_computation.11 | async-start | bytes 1835008 | tf_op jit(solution)/shard_map/psum | solution.py:43
  544.2 86.8 %reduce-scatter.12.cloned.1.call-start = ((), (), s32[]{:S(2)}) async-start(), calls=%async_computation.12 | async-start | bytes 2293760 | tf_op jit(solution)/shard_map/reduce_scatter | solution.py:59
  602.2 191.7 %copy-start.5 = (f32[1024,224]{0,1:T(8,128)}, f32[1024,224]{0,1:T(8,128)S(1)}, u32[]{:S(2)}) copy-start(f32[1024,224]{0,1:T(8,128)S(1)} %multiply_subtract_fusion) | copy-start | bytes 2752516
  602.2 41.6 %slice-start = ((s8[14680064]{0:T(1024)(128)(4,1)}), s8[2097152]{0:T(1024)(128)(4,1)S(1)}, s32[]{:S(2)}) async-start(s8[14680064]{0:T(1024)(128)(4,1)} %bitcast.63), calls=%async_computation.17 | async-start | bytes 4194304
  603.9 86.1 %reduce-scatter.14.cloned.1.call-start = ((), (), s32[]{:S(2)}) async-start(), calls=%async_computation.13 | async-start | bytes 655360 | tf_op jit(solution)/shard_map/reduce_scatter | solution.py:231
  658.7 10.6 %collective-permute-start.1 = (f32[1024,128]{0,1:T(8,128)S(1)}, f32[1024,128]{0,1:T(8,128)S(1)}, u32[]{:S(2)}, u32[]{:S(2)}) collective-permute-start(f32[1024,128]{0,1:T(8,128)S(1)} %pad_maximum_fusion.2), channel_id=1, source_target_pairs={{8,0},{16,8},{24,16},{32,24},{40,32},{48,40},{56,48},{64,56},{72,6... | collective-permute-start | bytes 1572872 | tf_op jit(solution)/shard_map/ppermute | solution.py:19
  670.2 78.5 %all-gather.4.cloned.1.call-start = ((), (), s32[]{:S(2)}) async-start(), calls=%async_computation.8 | async-start | bytes 6225920 | tf_op jit(solution)/shard_map/all_gather | solution.py:70
  671.0 77.7 %copy-start.22 = (bf16[2432,224]{0,1:T(8,128)(2,1)S(1)}, bf16[2432,224]{0,1:T(8,128)(2,1)}, u32[]{:S(2)}) copy-start(bf16[2432,224]{0,1:T(8,128)(2,1)} %param.24) | copy-start | bytes 3268612
  671.0 106.5 %all-gather.8.cloned.1.call-start = ((), (), s32[]{:S(2)}) async-start(), calls=%async_computation.14 | async-start | bytes 1474560 | tf_op jit(solution)/shard_map/all_gather | solution.py:81
  675.7 101.8 %copy-start.20 = (bf16[224,576]{1,0:T(8,128)(2,1)S(1)}, bf16[224,576]{1,0:T(8,128)(2,1)}, u32[]{:S(2)}) copy-start(bf16[224,576]{1,0:T(8,128)(2,1)} %param.18) | copy-start | bytes 774148
  692.6 88.0 %copy-start.17 = (bf16[1024,224]{0,1:T(8,128)(2,1)S(1)}, bf16[1024,224]{0,1:T(8,128)(2,1)}, u32[]{:S(2)}) copy-start(bf16[1024,224]{0,1:T(8,128)(2,1)} %param.25) | copy-start | bytes 1376260
  692.6 155.0 %all-reduce.14.cloned.1.call-start = ((), (), s32[]{:S(2)}) async-start(), calls=%async_computation.16 | async-start | bytes 3670016 | tf_op jit(solution)/shard_map/psum | solution.py:43
  780.3 253.0 %all-reduce.12.cloned.1.call-start = ((), (), s32[]{:S(2)}) async-start(), calls=%async_computation.15 | async-start | bytes 15138816 | tf_op jit(solution)/shard_map/psum | solution.py:259
  796.6 90.5 %copy-start.4 = (f32[1024,224]{0,1:T(8,128)S(1)}, f32[1024,224]{0,1:T(8,128)}, u32[]{:S(2)}) copy-start(f32[1024,224]{0,1:T(8,128)} %copy-done.3) | copy-start | bytes 2752516
  796.6 92.6 %copy-start.6 = (f32[1024,224]{0,1:T(8,128)S(1)}, f32[1024,224]{0,1:T(8,128)}, u32[]{:S(2)}) copy-start(f32[1024,224]{0,1:T(8,128)} %copy-done.5) | copy-start | bytes 2752516
  (26 other events, 210.2 us)
Sparse Core Ops, SparseCore 0:
  22.3 33.3 reduce-scatter.5
  112.0 48.3 all-reduce.7
  163.0 92.9 reduce-scatter.9
  258.5 173.0 reduce-scatter.7
  439.0 96.0 all-gather.5
  544.4 46.2 all-reduce.9
  604.0 26.9 reduce-scatter.11
  670.3 19.6 reduce-scatter.13
  692.3 56.2 all-gather.3
  750.8 26.5 all-gather.7
  780.4 67.1 all-reduce.13
  851.5 181.6 all-reduce.11
where the time goes:
time: 1050 us
  waiting for transfers between devices  790 us (75%)
  blocking collectives  87.5 us (8%)
  matrix products  82.2 us (8%)
  other arithmetic  49.1 us (5%)
  local copies, waits for them, and re-layouts  15.8 us (2%)
  between operations  14.8 us (1%)
    reduce_scatter x2, waiting for transfers between devices, project_rows(): lax.psum_scatter(jnp.concatenate([jnp.dot(normed, weight, preferred_eleme...  208 us
    psum x1, waiting for transfers between devices, body(): lax.psum((first_gain_grad, project_grad, bias_grad, output_grad, second_g...  142 us
    psum x3, waiting for transfers between devices, column_sum(): return lax.psum(values, 'col')  139 us
    all_gather x2, waiting for transfers between devices, fold_rows(): piece = lax.all_gather(grads, 'row', axis=0, tiled=True)  120 us
    reduce_scatter x2, waiting for transfers between devices, return_rows(): lax.psum_scatter(lax.dot_general(grads, weight, (((1,), (1,)), ((), ())),...  100 us
    all_gather x1, waiting for transfers between devices, spread_rows(): piece = lax.all_gather(values, 'row', axis=0, tiled=True)  56 us
    psum x4, blocking collectives, row_total(): return lax.psum(values, 'row')  37.3 us
    psum x1, blocking collectives, body(): lax.psum((first_gain_grad, project_grad, bias_grad, output_grad, second_g...  28.7 us
  transfers between devices with their start and end apart: 14, of which 14 were waited for; matrix products, arithmetic and copies ran while one was open for 5% of the time, Pallas kernels for 0%

commit v1 on v0

v1 whole, which is shorter than its diff:
```python
import functools

import jax
import jax.numpy as jnp
from jax import lax
from jax.experimental import pallas as pl
from jax.experimental.pallas import tpu as pltpu
from jax.sharding import PartitionSpec as P

D = 896
HEADS = 14
GROUPS = 2
HEAD_DIM = 64
MAXLEN = 1024
EPS = 1e-06
BF = jnp.bfloat16
F32 = jnp.float32
ROWS = 4
FEAT = 224
SHARE = 256
SHARD = 1024
HALF_FF = 2432
WIN = 640
LAST = HALF_FF - WIN
PADF = 256
VMEM_LIMIT = 60 * 1024 * 1024


def from_behind(block, axis, distance):
    devices = range(lax.axis_size(axis))
    route = [(i - distance, i) for i in devices if i - distance in devices]
    return lax.ppermute(block, axis, route)


def rotate(values, cosine, sine):
    half = HEAD_DIM // 2
    if values.ndim == 3:
        cosine = cosine[:, None, :]
        sine = sine[:, None, :]
    first = values[..., :half]
    second = values[..., half:]
    return jnp.concatenate(
        [first * cosine - second * sine, second * cosine + first * sine], axis=-1
    )


def dot(a, b):
    return jnp.dot(a, b, preferred_element_type=F32)


def dot_nt(a, b):
    return lax.dot_general(a, b, (((1,), (1,)), ((), ())), preferred_element_type=F32)


def dot_tn(a, b):
    return lax.dot_general(a, b, (((0,), (0,)), ((), ())), preferred_element_type=F32)


def rcopy(src, dst, send, recv, **device):
    return pltpu.make_async_remote_copy(
        src_ref=src,
        dst_ref=dst,
        send_sem=send,
        recv_sem=recv,
        device_id=device,
        device_id_type=pl.DeviceIdType.MESH,
    )


def greet(peers):
    barrier = pltpu.get_barrier_semaphore()
    for peer in peers:
        pl.semaphore_signal(
            barrier, inc=1, device_id=peer, device_id_type=pl.DeviceIdType.MESH
        )
    pl.semaphore_wait(barrier, len(peers))


def vmem_call(kernel, inputs, outs, scratch, collective, cost=None):
    return pl.pallas_call(
        kernel,
        out_shape=outs,
        in_specs=[pl.BlockSpec(memory_space=pltpu.VMEM)] * inputs,
        out_specs=jax.tree.map(lambda _: pl.BlockSpec(memory_space=pltpu.VMEM), outs),
        scratch_shapes=scratch,
        compiler_params=pltpu.CompilerParams(
            collective_id=collective,
            has_side_effects=True,
            vmem_limit_bytes=VMEM_LIMIT,
        ),
        cost_estimate=cost,
    )


def grads_kernel(
    count,
    joined,
    g_ref,
    out_ref,
    core_in,
    part,
    part_low,
    x_in,
    y_in,
    mine,
    z_in,
    sem_core,
    sem_x,
    sem_y,
    sem_z,
    sem_gy,
    sem_gx,
    sem_gc,
):
    d = lax.axis_index("dp")
    r = lax.axis_index("row")
    core = lax.rem(d, 2)
    y = lax.rem(d // 2, 2)
    x = d // 4
    other_core = d + 1 - 2 * core
    other_y = d + 2 - 4 * y

    def x_peer(k):
        return lax.rem(x + k, 4) * 4 + y * 2 + core

    greet(
        [{"dp": other_core}, {"dp": other_y}]
        + [{"dp": x_peer(k)} for k in (1, 2, 3)]
        + [{"row": lax.rem(r + k, 4)} for k in (1, 2, 3)]
    )
    rows = lambda start, size: pl.ds(pl.multiple_of(start, 16), size)
    pending = []

    def go(*args, **device):
        copy = rcopy(*args, **device)
        copy.start()
        pending.append(copy)
        return copy

    first = [
        go(
            g_ref.at[t, :, rows((1 - core) * 128, 128), :],
            core_in.at[t],
            sem_core.at[0, t],
            sem_core.at[1, t],
            dp=other_core,
        )
        for t in range(count)
    ]
    second = []
    for t in range(count):
        first[t].wait_recv()
        total = g_ref[t, :, rows(core * 128, 128), :].astype(F32) + core_in[t].astype(F32)
        part[t] = total
        part_low[t, :, 0:128, :] = total.astype(BF)
        second.append(
            [
                go(
                    part_low.at[t, :, rows(lax.rem(x + k, 4) * 32, 32), :],
                    x_in.at[t, k - 1],
                    sem_x.at[0, t, k - 1],
                    sem_x.at[1, t, k - 1],
                    dp=x_peer(k),
                )
                for k in (1, 2, 3)
            ]
        )
    third = []
    for t in range(count):
        total = part[t, :, rows(x * 32, 32), :]
        for k in (1, 2, 3):
            second[t][k - 1].wait_recv()
            total = total + x_in[t, k - 1].astype(F32)
        part[t, :, 0:32, :] = total
        part_low[t, :, 128:160, :] = total.astype(BF)
        third.append(
            go(
                part_low.at[t, :, rows(128 + (1 - y) * 16, 16), :],
                y_in.at[t],
                sem_y.at[0, t],
                sem_y.at[1, t],
                dp=other_y,
            )
        )
    fourth = []
    for t in range(count):
        third[t].wait_recv()
        total = part[t, :, rows(y * 16, 16), :] + y_in[t].astype(F32)
        mine[t] = total.astype(BF)
        fourth.append(
            [
                go(
                    mine.at[t, lax.rem(r + k, 4)],
                    z_in.at[t, r],
                    sem_z.at[0, t, k - 1],
                    sem_z.at[1, t, k - 1],
                    row=lax.rem(r + k, 4),
                )
                for k in (1, 2, 3)
            ]
        )
    own = core * 128 + x * 32 + y * 16
    gather = []
    for t in range(count):
        z_in[t, r] = mine[t, r]
        for k in (1, 2, 3):
            fourth[t][k - 1].wait_recv()
        if joined:
            for q in range(3):
                out_ref[t, rows(own, 16), q * WIN : (q + 1) * WIN] = z_in[t, q]
            out_ref[t, rows(own, 16), 3 * WIN : HALF_FF] = z_in[t, 3][:, 4 * WIN - HALF_FF :]
        else:
            total = z_in[t, 0].astype(F32)
            for q in range(1, 4):
                total = total + z_in[t, q].astype(F32)
            out_ref[t, rows(own, 16), :] = total.astype(BF)
        block = out_ref.at[t, rows(own, 16), :]
        gather.append(go(block, block, sem_gy.at[0, t], sem_gy.at[1, t], dp=other_y))
    wide = core * 128 + x * 32
    spread = []
    for t in range(count):
        gather[t].wait_recv()
        block = out_ref.at[t, rows(wide, 32), :]
        spread.append(
            [
                go(
                    block,
                    block,
                    sem_gx.at[0, t, k - 1],
                    sem_gx.at[1, t, k - 1],
                    dp=x_peer(k),
                )
                for k in (1, 2, 3)
            ]
        )
    last = []
    for t in range(count):
        for k in (1, 2, 3):
            spread[t][k - 1].wait_recv()
        block = out_ref.at[t, rows(core * 128, 128), :]
        last.append(go(block, block, sem_gc.at[0, t], sem_gc.at[1, t], dp=other_core))
    for t in range(count):
        last[t].wait_recv()
    for copy in pending:
        copy.wait_send()


def sum_grads(grads, joined, collective):
    count = grads.shape[0]
    width = grads.shape[3]
    out_width = HALF_FF if joined else width
    dma = pltpu.SemaphoreType.DMA
    return vmem_call(
        functools.partial(grads_kernel, count, joined),
        1,
        jax.ShapeDtypeStruct((count, PADF, out_width), BF),
        [
            pltpu.VMEM((count, 4, 128, width), BF),
            pltpu.VMEM((count, 4, 128, width), F32),
            pltpu.VMEM((count, 4, 160, width), BF),
            pltpu.VMEM((count, 3, 4, 32, width), BF),
            pltpu.VMEM((count, 4, 16, width), BF),
            pltpu.VMEM((count, 4, 16, width), BF),
            pltpu.VMEM((count, 4, 16, width), BF),
            dma((2, count)),
            dma((2, count, 3)),
            dma((2, count)),
            dma((2, count, 3)),
            dma((2, count)),
            dma((2, count, 3)),
            dma((2, count)),
        ],
        collective,
    )(grads)


def ffn_kernel(
    ns_ref,
    cot_ref,
    gate_ref,
    up_ref,
    down_ref,
    mid_ref,
    second_ref,
    block_ref,
    grads_ref,
    ns_all,
    hid,
    gg,
    gu,
    sp_send,
    sp_in,
    op_send,
    op_in,
    cs_send,
    cs_in,
    co_send,
    co_in,
    sem_ag,
    sem_sp,
    sem_op,
    sem_cs,
    sem_co,
):
    r = lax.axis_index("row")
    c = lax.axis_index("col")
    greet([{"row": lax.rem(r + k, 4)} for k in (1, 2, 3)] + [{"col": 1 - c}])
    pending = []

    def go(*args, **device):
        copy = rcopy(*args, **device)
        copy.start()
        pending.append(copy)
        return copy

    span = lambda q: pl.ds(pl.multiple_of(q * SHARE, SHARE), SHARE)
    incoming = [
        go(
            ns_ref,
            ns_all.at[:, span(r), :],
            sem_ag.at[0, k - 1],
            sem_ag.at[1, k - 1],
            row=lax.rem(r + k, 4),
        )
        for k in (1, 2, 3)
    ]
    ns_all[:, span(r), :] = ns_ref[...]
    back = []
    for k in range(4):
        q = lax.rem(r + 4 - k, 4)
        grad_hidden = dot_nt(cot_ref[0, span(q), :], down_ref[0])
        for j in range(1, 4):
            grad_hidden += dot_nt(cot_ref[j, span(q), :], down_ref[j])
        if k:
            incoming[k - 1].wait_recv()
        gate = dot(ns_all[0, span(q), :], gate_ref[0])
        up = dot(ns_all[0, span(q), :], up_ref[0])
        for j in range(1, 4):
            gate += dot(ns_all[j, span(q), :], gate_ref[j])
            up += dot(ns_all[j, span(q), :], up_ref[j])
        sigma = 1.0 / (1.0 + jnp.exp(-gate))
        silu = gate * sigma
        hid[span(q), :] = (silu * up).astype(BF)
        g_gate = (grad_hidden * up * (sigma + silu * (1.0 - sigma))).astype(BF)
        g_up = (grad_hidden * silu).astype(BF)
        gg[span(q), :] = g_gate
        gu[span(q), :] = g_up
        for j in range(4):
            sp_send[k, j] = (
                dot_nt(g_gate, gate_ref[j]) + dot_nt(g_up, up_ref[j])
            ).astype(BF)
        if k:
            back.append(
                go(
                    sp_send.at[k],
                    sp_in.at[k - 1],
                    sem_sp.at[0, k - 1],
                    sem_sp.at[1, k - 1],
                    row=q,
                )
            )
    outgoing = []
    for k in (1, 2, 3, 0):
        j = lax.rem(r + k, 4)
        for q in range(4):
            op_send[j, q * SHARE : (q + 1) * SHARE, :] = dot(
                hid[q * SHARE : (q + 1) * SHARE, :], down_ref[j]
            ).astype(BF)
        op_send[j, span(r), :] = (
            op_send[j, span(r), :].astype(F32) + 0.5 * mid_ref[j]
        ).astype(BF)
        if k:
            outgoing.append(
                go(
                    op_send.at[j],
                    op_in.at[k - 1],
                    sem_op.at[0, k - 1],
                    sem_op.at[1, k - 1],
                    row=j,
                )
            )
    total = sp_send[0].astype(F32)
    for k in (1, 2, 3):
        back[k - 1].wait_recv()
        total += sp_in[k - 1].astype(F32)
    cs_send[...] = total.astype(BF)
    cross = go(cs_send, cs_in, sem_cs.at[0], sem_cs.at[1], col=1 - c)
    grads_ref[:, :, FEAT:PADF, :] = jnp.zeros((3, 4, PADF - FEAT, WIN), BF)
    for j in range(4):
        grads_ref[0, j, 0:FEAT, :] = dot_tn(ns_all[j], gg[...]).astype(BF)
        grads_ref[1, j, 0:FEAT, :] = dot_tn(ns_all[j], gu[...]).astype(BF)
        grads_ref[2, j, 0:FEAT, :] = dot_tn(cot_ref[j], hid[...]).astype(BF)
    total = op_send[r].astype(F32)
    for k in (1, 2, 3):
        outgoing[k - 1].wait_recv()
        total += op_in[k - 1].astype(F32)
    co_send[...] = total.astype(BF)
    final = go(co_send, co_in, sem_co.at[0], sem_co.at[1], col=1 - c)
    cross.wait_recv()
    second_ref[...] = cs_send[...].astype(F32) + cs_in[...].astype(F32)
    final.wait_recv()
    block_ref[...] = (co_send[...].astype(F32) + co_in[...].astype(F32)).astype(BF)
    for copy in pending:
        copy.wait_send()


def feed_forward(ns, cot_all, gate_full, up_full, down_full, middle):
    dma = pltpu.SemaphoreType.DMA
    blocked = pltpu.VMEM((4, SHARE, FEAT), BF)
    return vmem_call(
        ffn_kernel,
        6,
        (
            jax.ShapeDtypeStruct((4, SHARE, FEAT), F32),
            jax.ShapeDtypeStruct((SHARD, FEAT), BF),
            jax.ShapeDtypeStruct((3, 4, PADF, WIN), BF),
        ),
        [
            pltpu.VMEM((4, SHARD, FEAT), BF),
            pltpu.VMEM((SHARD, WIN), BF),
            pltpu.VMEM((SHARD, WIN), BF),
            pltpu.VMEM((SHARD, WIN), BF),
            pltpu.VMEM((4, 4, SHARE, FEAT), BF),
            pltpu.VMEM((3, 4, SHARE, FEAT), BF),
            pltpu.VMEM((4, SHARD, FEAT), BF),
            pltpu.VMEM((3, SHARD, FEAT), BF),
            blocked,
            blocked,
            pltpu.VMEM((SHARD, FEAT), BF),
            pltpu.VMEM((SHARD, FEAT), BF),
            dma((2, 3)),
            dma((2, 3)),
            dma((2, 3)),
            dma((2,)),
            dma((2,)),
        ],
        1,
        pl.CostEstimate(flops=12 * 10**9, bytes_accessed=16 * 10**6, transcendentals=10**6),
    )(ns, cot_all, gate_full, up_full, down_full, middle)


def col_sum(values):
    own = values.astype(BF)
    other = lax.ppermute(own, "col", [(0, 1), (1, 0)])
    return own.astype(F32) + other.astype(F32)


def masked_scores(queries, key_part, allowed):
    scores = (
        jnp.einsum("qmd,kd->mqk", queries, key_part, preferred_element_type=F32)
        * HEAD_DIM ** (-0.5)
    )
    return jnp.where(allowed[None], scores, -1e30)


def attend_forward(queries, pairs, allowed):
    scores = masked_scores(queries, pairs[:, :HEAD_DIM], allowed)
    peak = jnp.max(scores, axis=-1, keepdims=True)
    powered = jnp.exp(scores - peak)
    denominator = jnp.sum(powered, axis=-1, keepdims=True)
    probs = (powered / denominator).astype(BF)
    mixed = jnp.einsum(
        "mqk,kd->qmd", probs, pairs[:, HEAD_DIM:], preferred_element_type=F32
    )
    return (mixed, peak + jnp.log(denominator))


def attend_backward(queries, pairs, allowed, log_total, grad_mixed):
    key_part = pairs[:, :HEAD_DIM]
    value_part = pairs[:, HEAD_DIM:]
    scores = masked_scores(queries, key_part, allowed)
    probs = jnp.exp(scores - log_total)
    probs_low = probs.astype(BF)
    grad_values = jnp.einsum(
        "mqk,qmd->kd", probs_low, grad_mixed, preferred_element_type=F32
    )
    grad_probs = jnp.einsum(
        "qmd,kd->mqk", grad_mixed, value_part, preferred_element_type=F32
    )
    inner_sum = jnp.sum(probs * grad_probs, axis=-1, keepdims=True)
    grad_scores = (probs * (grad_probs - inner_sum)).astype(BF)
    grad_queries = (
        jnp.einsum("mqk,kd->qmd", grad_scores, key_part, preferred_element_type=F32)
        * HEAD_DIM ** (-0.5)
    )
    grad_keys = (
        jnp.einsum("mqk,qmd->kd", grad_scores, queries, preferred_element_type=F32)
        * HEAD_DIM ** (-0.5)
    )
    return (grad_queries, jnp.concatenate([grad_keys, grad_values], axis=1))


def windows(weight, axis):
    return jnp.stack(
        [
            lax.slice_in_dim(weight, min(WIN * q, LAST), min(WIN * q, LAST) + WIN, axis=axis)
            for q in range(ROWS)
        ]
    )


def exchange(blocks):
    return lax.all_to_all(blocks, "row", 0, 0, tiled=True)


def body(
    activations,
    starts,
    first_gain,
    project_weight,
    project_bias,
    output_weight,
    second_gain,
    gate_weight,
    up_weight,
    down_weight,
    cotangent,
):
    window = MAXLEN + SHARE
    r = lax.axis_index("row")
    shard = lax.axis_index("dp")
    group_heads = HEADS // GROUPS
    query_width = group_heads * HEAD_DIM

    x_low = exchange(activations.reshape(ROWS, SHARE, FEAT))
    gains = lax.all_gather(jnp.stack([first_gain, second_gain]), "row")
    gain_one = gains[:, 0][:, None, :]
    gain_two = gains[:, 1][:, None, :]
    project_full = lax.all_gather(project_weight, "row")
    output_full = lax.all_gather(output_weight, "row")
    live = (jnp.arange(WIN) >= 4 * WIN - HALF_FF) | (r < 3)
    gate_full = jnp.where(live, exchange(windows(gate_weight, 1)), 0).astype(BF)
    up_full = jnp.where(live, exchange(windows(up_weight, 1)), 0).astype(BF)
    down_full = exchange(windows(down_weight, 0))
    cot_all = lax.all_gather(cotangent, "row")

    local_index = r * SHARE + jnp.arange(SHARE, dtype=jnp.int32)
    start_local = (
        lax.dynamic_slice_in_dim(starts, r * SHARE, SHARE, 0) - shard * SHARD
    )
    positions = (local_index - start_local).astype(F32)
    half = HEAD_DIM // 2
    freqs = 1000000.0 ** (-jnp.arange(half, dtype=F32) * 2.0 / HEAD_DIM)
    angle = positions[:, None] * freqs[None, :]
    cosine, sine = jnp.cos(angle), jnp.sin(angle)
    key_local = r * SHARE - MAXLEN + jnp.arange(window, dtype=jnp.int32)
    allowed = (key_local[None, :] >= start_local[:, None]) & (
        key_local[None, :] <= local_index[:, None]
    )

    x = x_low.astype(F32)
    first_rate = lax.rsqrt(jnp.mean(x * x, axis=(0, 2))[None, :, None] + EPS)
    normed_first = (x * first_rate * gain_one).astype(BF)
    projected = (
        jnp.einsum("jtf,jfn->tn", normed_first, project_full, preferred_element_type=F32)
        + project_bias
    )
    queries = rotate(
        projected[:, :query_width].reshape(SHARE, group_heads, HEAD_DIM), cosine, sine
    ).astype(BF)
    keys_new = rotate(projected[:, query_width : query_width + HEAD_DIM], cosine, sine)
    pair_share = jnp.concatenate(
        [keys_new, projected[:, query_width + HEAD_DIM :]], axis=1
    ).astype(BF)
    shard_pairs = lax.all_gather(pair_share, "row", axis=0, tiled=True)
    earlier = from_behind(shard_pairs, "dp", 1)
    pairs = lax.dynamic_slice_in_dim(
        jnp.concatenate([earlier, shard_pairs], axis=0), r * SHARE, window, 0
    )
    mixed, log_total = attend_forward(queries, pairs, allowed)
    attended = mixed.reshape(SHARE, query_width).astype(BF)
    middle = x + col_sum(
        jnp.einsum("th,jhf->jtf", attended, output_full, preferred_element_type=F32)
    )
    second_rate = lax.rsqrt(jnp.mean(middle * middle, axis=(0, 2))[None, :, None] + EPS)
    normed_second = (middle * second_rate * gain_two).astype(BF)

    grad_second, block_output, ff_grads = feed_forward(
        normed_second, cot_all, gate_full, up_full, down_full, middle
    )

    cot_own = lax.dynamic_slice_in_dim(cot_all, r * SHARE, SHARE, 1).astype(F32)
    weighted_second = grad_second * gain_two
    second_inner = jnp.sum(weighted_second * middle, axis=(0, 2))[None, :, None]
    second_gain_grad = jnp.sum(grad_second * middle * second_rate, axis=1)
    grad_middle = (
        cot_own
        + second_rate * weighted_second
        - middle * (second_rate**3 * second_inner / D)
    )
    grad_branch = grad_middle.astype(BF)
    grad_attended = (
        jnp.einsum("jtf,jhf->th", grad_branch, output_full, preferred_element_type=F32)
        .astype(BF)
        .reshape(SHARE, group_heads, HEAD_DIM)
    )
    grad_queries, grad_pairs = attend_backward(
        queries, pairs, allowed, log_total, grad_attended
    )
    grad_wide = lax.dynamic_update_slice(
        jnp.zeros((MAXLEN + SHARD, 2 * HEAD_DIM), F32), grad_pairs, (r * SHARE, 0)
    )
    returned = from_behind(grad_wide[:MAXLEN].astype(BF), "dp", -1)
    own_pairs = (grad_wide[MAXLEN:] + returned.astype(F32)).astype(BF)
    grad_pair = lax.psum_scatter(
        own_pairs, "row", scatter_dimension=0, tiled=True
    ).astype(F32)
    grad_keys = rotate(grad_pair[:, :HEAD_DIM], cosine, -sine)
    grad_query_plain = rotate(grad_queries, cosine, -sine).reshape(SHARE, query_width)
    grad_projected = jnp.concatenate(
        [grad_query_plain, grad_keys, grad_pair[:, HEAD_DIM:]], axis=1
    ).astype(BF)
    grad_first = col_sum(
        jnp.einsum("tn,jfn->jtf", grad_projected, project_full, preferred_element_type=F32)
    )
    weighted_first = grad_first * gain_one
    first_inner = jnp.sum(weighted_first * x, axis=(0, 2))[None, :, None]
    first_gain_grad = jnp.sum(grad_first * x * first_rate, axis=1)
    input_own = (
        grad_middle
        + first_rate * weighted_first
        - x * (first_rate**3 * first_inner / D)
    )
    input_grad = exchange(input_own.astype(BF)).reshape(SHARD, FEAT).astype(F32)

    ff_sum = sum_grads(ff_grads, True, 2)[:, :FEAT].astype(F32)
    width = project_weight.shape[1]
    at_grads = jnp.concatenate(
        [
            jnp.einsum("jtf,tn->jfn", normed_first, grad_projected, preferred_element_type=F32),
            jnp.einsum("jtf,th->jfh", grad_branch, attended, preferred_element_type=F32),
        ],
        axis=2,
    ).astype(BF)
    at_grads = jnp.pad(at_grads, ((0, 0), (0, PADF - FEAT), (0, 0)))
    at_sum = sum_grads(at_grads[None], False, 3)[0, :FEAT].astype(F32)
    bias_grad = jnp.sum(grad_projected.astype(F32), axis=0)
    small = lax.psum(
        jnp.concatenate([first_gain_grad.ravel(), second_gain_grad.ravel(), bias_grad]),
        ("dp", "row"),
    )
    first_gain_grad = lax.dynamic_slice_in_dim(small[:D], r * FEAT, FEAT, 0)
    second_gain_grad = lax.dynamic_slice_in_dim(small[D : 2 * D], r * FEAT, FEAT, 0)
    bias_grad = small[2 * D :]
    return (
        block_output,
        input_grad,
        first_gain_grad,
        at_sum[:, :width],
        bias_grad,
        at_sum[:, width:].T,
        second_gain_grad,
        ff_sum[0],
        ff_sum[1],
        ff_sum[2].T,
    )


def solution(mesh):
    return jax.shard_map(
        body,
        mesh=mesh,
        in_specs=(
            P("dp", "row"),
            P("dp"),
            P("row"),
            P("row", "col"),
            P("col"),
            P("col", "row"),
            P("row"),
            P("row", "col"),
            P("row", "col"),
            P("col", "row"),
            P("dp", "row"),
        ),
        out_specs=(
            P("dp", "row"),
            P("dp", "row"),
            P("row"),
            P("row", "col"),
            P("col"),
            P("col", "row"),
            P("row"),
            P("row", "col"),
            P("row", "col"),
            P("col", "row"),
        ),
        check_vma=False,
    )
```

time: 1050 us -> 742 us (0.71); the launches traced: 1050 us -> 727 us
  waiting for transfers between devices: 790 us -> 39.4 us
  blocking collectives: 87.5 us -> 326 us
  Pallas kernels: 0 us -> 193 us
  matrix products: 82.2 us -> 29.2 us
  starting transfers between devices: 10.2 us -> 48.1 us
  local copies, waits for them, and re-layouts: 15.8 us -> 32.4 us
    reduce_scatter x4 -> x0, waiting for transfers between devices: 308 us -> none  [the longest x2 208 us: project_rows(): lax.psum_scatter(jnp.concatenate([jnp.dot(normed, weight, preferred_eleme...]
    psum x4 -> x0, waiting for transfers between devices: 280 us -> none  [the longest x1 142 us: body(): lax.psum((first_gain_grad, project_grad, bias_grad, output_grad, second_g...]
    psum x5 -> x1, blocking collectives: 65.9 us -> 273 us  [body(): lax.psum(jnp.concatenate([first_gain_grad.ravel(), second_gain_grad.ravel...]
    pallas_call x0 -> x3, Pallas kernels: none -> 193 us  [the longest x2 101 us: sum_grads(): vmem_call(functools.partial(grads_kernel, count, joined), 1, jax.ShapeDty...]
    all_gather x3 -> x1, waiting for transfers between devices: 176 us -> 0.01 us  [body(): cot_all = lax.all_gather(cotangent, 'row')]
    dot_general x19 -> x9, matrix products: 63.7 us -> 15.5 us  [the longest x1 3.81 us: attend_backward(): jnp.einsum('mqk,qmd->kd', grad_scores, queries, preferred_element_type=F32)]
    all_gather x1 -> x3, blocking collectives: 12.2 us -> 40.2 us  [the longest x1 19.6 us: body(): project_full = lax.all_gather(project_weight, 'row')]
    all_to_all x0 -> x5, starting transfers between devices: none -> 21.8 us  [exchange(): return lax.all_to_all(blocks, 'row', 0, 0, tiled=True)]
  transfers between devices with their start and end apart: 14 -> 11, of which waited for: 14 -> 5; matrix products, arithmetic and copies ran while one was open for 5% -> 8% of each run, Pallas kernels for 0% -> 8%
where the time goes in v1:
time: 742 us; the launch traced here: 727 us
  blocking collectives  326 us (44%)
  Pallas kernels  193 us (26%)
  starting transfers between devices  48.1 us (6%)
  other arithmetic  44.5 us (6%)
  waiting for transfers between devices  39.4 us (5%)
  local copies, waits for them, and re-layouts  32.4 us (4%)
  matrix products  29.2 us (4%)
  between operations  15.2 us (2%)
    psum x1, blocking collectives, body(): lax.psum(jnp.concatenate([first_gain_grad.ravel(), second_gain_grad.ravel...  273 us
    pallas_call x2, Pallas kernels, sum_grads(): vmem_call(functools.partial(grads_kernel, count, joined), 1, jax.ShapeDty...  101 us
    pallas_call x1, Pallas kernels, feed_forward(): vmem_call(ffn_kernel, 6, (jax.ShapeDtypeStruct((4, SHARE, FEAT), F32), ja...  91.5 us
    all_to_all x5, starting transfers between devices, exchange(): return lax.all_to_all(blocks, 'row', 0, 0, tiled=True)  21.8 us
    ppermute x2, starting transfers between devices, from_behind(): return lax.ppermute(block, axis, route)  20.4 us
    all_gather x1, blocking collectives, body(): project_full = lax.all_gather(project_weight, 'row')  19.6 us
  transfers between devices with their start and end apart: 11, of which 5 were waited for; matrix products, arithmetic and copies ran while one was open for 8% of the time, Pallas kernels for 8%

profile of v1, /device:TPU:1, one launch (start us, length us, event | category | flops | bytes accessed | tf_op | source)
XLA Modules:
  0.0 727.4 jit_solution(5181900906110488460)
XLA Ops:
  9.1 5.9 all-to-all-start
  16.3 9.4 %all-gather.4 = f32[4,2,224]{2,1,0:T(2,128)S(1)} all-gather(f32[1,2,224]{2,1,0:T(2,128)S(1)} %maximum_bitcast_fusion), channel_id=2, replica_groups=mesh['dp'=16,'row'=4,'col'=2] {'row'}, dimensions={0}, use_global_device_ids=true | all-gather | bytes 8960 | tf_op jit(solution)/shard_map/all_gather | solution.py:526
  26.3 19.6 %all-gather.1 = bf16[896,576]{1,0:T(8,128)(2,1)} all-gather(bf16[224,576]{1,0:T(8,128)(2,1)S(1)} %copy-done.20), channel_id=3, replica_groups=mesh['dp'=16,'row'=4,'col'=2] {'row'}, dimensions={0}, use_global_device_ids=true | all-gather | bytes 1290240 | tf_op jit(solution)/shard_map/all_gather | solution.py:529
  55.6 11.2 %all-gather.2 = bf16[1792,224]{1,0:T(8,128)(2,1)S(1)} all-gather(bf16[448,224]{1,0:T(8,128)(2,1)S(1)} %copy-done.21), channel_id=4, replica_groups=mesh['dp'=16,'row'=4,'col'=2] {'row'}, dimensions={0}, use_global_device_ids=true | all-gather | bytes 1003520 | tf_op jit(solution)/shard_map/all_gather | solution.py:530
  66.8 3.7 all-to-all-start.1
  74.4 12.7 %all_gather.31 = bf16[1024,128]{0,1:T(8,128)(2,1)} all-gather(bf16[256,128]{0,1:T(8,128)(2,1)S(1)} %pad_maximum_fusion.8), channel_id=1, replica_groups=mesh['dp'=16,'row'=4,'col'=2] {'row'}, dimensions={0}, use_global_device_ids=true | all-gather | bytes 327680 | tf_op jit(solution)/shard_map/all_gather | solution.py:565
  87.1 14.5 %collective-permute-start = (bf16[1024,128]{0,1:T(8,128)(2,1)}, bf16[1024,128]{0,1:T(8,128)(2,1)}, u32[]{:S(2)}, u32[]{:S(2)}) collective-permute-start(bf16[1024,128]{0,1:T(8,128)(2,1)} %all_gather.31), channel_id=1, source_target_pairs={{0,8},{8,16},{16,24},{24,32},{32,40},{40,48},{48,56},{56,64},{64,7... | collective-permute-start | bytes 786440 | tf_op jit(solution)/shard_map/ppermute | solution.py:32
  107.1 4.3 all-to-all-start.3
  111.3 2.7 fusion.63
  114.1 3.6 copy-done
  118.8 8.3 %all-to-all-done.3 = bf16[4,640,224]{1,2,0:T(8,128)(2,1)} async-done(((bf16[4,640,224]{1,2,0:T(8,128)(2,1)}), bf16[4,640,224]{1,2,0:T(8,128)(2,1)}, u32[]{:S(2)}, u32[]{:S(2)}) %all-to-all-start.3) | async-done | bytes 1146912 | tf_op jit(solution)/shard_map/all_to_all | solution.py:503
  127.2 4.3 all-to-all-start.2
  131.5 5.4 fusion.20
  139.6 3.1 collective-permute-start.1
  145.0 2.7 all-to-all-done.2
  147.7 2.9 broadcast_select_fusion
  150.6 4.1 collective-permute-done.1
  157.3 4.1 copy.110
  161.4 91.5 %shard_map.186 = (f32[4,256,224]{2,1,0:T(8,128)}, bf16[1024,224]{1,0:T(8,128)(2,1)}, bf16[3,4,256,640]{3,2,1,0:T(8,128)(2,1)}) custom-call(bf16[4,256,224]{2,1,0:T(8,128)(2,1)} %multiply_convert_fusion.ns_ref, bf16[4,1024,224]{2,1,0:T(8,128)(2,1)} %bitcast.139, bf16[4,224,640]{2,1,0:T(8,128)(2,1)} %get-tuple-element.107.gate_ref, ...), custom_call_target="tpu_custom_call" | custom-call | flops 12000000000 | bytes 16000000 | tf_op jit(solution)/shard_map/pallas_call | solution.py:410
  257.0 8.0 %fusion = (f32[7,256]{1,0:T(8,128)S(1)}, f32[1280,256,7]{1,0,2:T(8,128)}) fusion(f32[7,256,1280]{1,2,0:T(8,128)} %copy-done, f32[7,256]{1,0:T(8,128)S(1)} %log_add_fusion, bf16[256,7,64]{0,2,1:T(8,128)(2,1)S(1)} %bitcast.142, bf16[1280,128]{0,1:T(8,128)(2,1)S(1)} %copy-done.4), kind=kOutput, calls=%fused_computation.2 | convolution fusion | flops 300480768 | bytes 18758656 | tf_op jit(solution)/shard_map/qmd,kd->mqk/dot_general | solution.py:477
  267.7 10.1 %fusion.2 = bf16[7,256,1280]{1,2,0:T(8,128)(2,1)} fusion(f32[1280,256,7]{1,0,2:T(8,128)} %get-tuple-element.111, f32[7,256,1280]{1,2,0:T(8,128)} %copy-done, f32[7,256]{1,0:T(8,128)S(1)} %get-tuple-element.110, f32[7,256]{1,0:T(8,128)S(1)} %log_add_fusion), kind=kLoop, calls=%fused_computation.4 | loop fusion | flops 9175040 | bytes 22951936 | tf_op jit(solution)/shard_map/convert_element_type | solution.py:481
  277.8 3.8 fusion.14
  282.5 5.9 collective-permute-start.2
  288.5 60.9 %shard_map.188 = bf16[3,256,2432]{2,1,0:T(8,128)(2,1)} custom-call(bf16[3,4,256,640]{3,2,1,0:T(8,128)(2,1)} %get-tuple-element.15.g_ref), custom_call_target="tpu_custom_call" | custom-call | tf_op jit(solution)/shard_map/pallas_call | solution.py:253
  351.9 2.9 slice_bitcast_fusion
  356.9 3.2 fusion.17
  362.5 14.7 %reduce-scatter.2.cloned.1.call-done = bf16[256,128]{0,1:T(8,128)(2,1)} async-done(((bf16[1024,128]{0,1:T(8,128)(2,1)}), bf16[256,128]{0,1:T(8,128)(2,1)}) %reduce-scatter.2.cloned.1.call-update) | async-done | bytes 65552 | tf_op jit(solution)/shard_map/reduce_scatter | solution.py:605
  383.0 40.1 %shard_map.187 = bf16[1,256,1024]{2,1,0:T(8,128)(2,1)} custom-call(bf16[1,4,256,1024]{3,2,1,0:T(8,128)(2,1)} %fusion.16.g_ref), custom_call_target="tpu_custom_call" | custom-call | tf_op jit(solution)/shard_map/pallas_call | solution.py:253
  423.3 2.8 collective-permute-start.3
  429.5 8.9 %collective-permute-done.3 = bf16[4,256,224]{2,1,0:T(8,128)(2,1)S(1)} collective-permute-done((bf16[4,256,224]{2,1,0:T(8,128)(2,1)S(1)}, bf16[4,256,224]{2,1,0:T(8,128)(2,1)S(1)}, u32[]{:S(2)}, u32[]{:S(2)}) %collective-permute-start.3) | collective-permute-done | bytes 458784 | tf_op jit(solution)/shard_map/ppermute | solution.py:444
  440.2 3.7 all-to-all-start.4
  443.9 273.2 %psum.7 = f32[2368]{0:T(1024)S(1)} all-reduce(f32[2368]{0:T(1024)S(1)} %pad_maximum_fusion.9), channel_id=1, replica_groups=mesh['dp'=16,'row'=4,'col'=2] {'dp','row'}, use_global_device_ids=true, to_apply=%region_11.12 | all-reduce | flops 2368 | bytes 18944 | tf_op jit(solution)/shard_map/psum | solution.py:638
  (180 shorter events, 60.3 us)
Async XLA Ops:
  7.2 9.1 %copy-start.42 = (f32[224]{0:T(256)S(1)}, f32[224]{0:T(256)}, u32[]{:S(2)}) copy-start(f32[224]{0:T(256)} %param.13) | copy-start | bytes 2692
  7.2 9.1 %copy-start.41 = (f32[224]{0:T(256)S(1)}, f32[224]{0:T(256)}, u32[]{:S(2)}) copy-start(f32[224]{0:T(256)} %param.17) | copy-start | bytes 2692
  7.2 19.1 %copy-start.20 = (bf16[224,576]{1,0:T(8,128)(2,1)S(1)}, bf16[224,576]{1,0:T(8,128)(2,1)}, u32[]{:S(2)}) copy-start(bf16[224,576]{1,0:T(8,128)(2,1)} %param.14) | copy-start | bytes 774148
  7.2 39.3 %copy-start.6 = (bf16[224,2432]{1,0:T(8,128)(2,1)S(1)}, bf16[224,2432]{1,0:T(8,128)(2,1)}, u32[]{:S(2)}) copy-start(bf16[224,2432]{1,0:T(8,128)(2,1)} %param.18) | copy-start | bytes 3268612
  9.1 57.7 %all-to-all-start = ((bf16[4,256,224]{1,2,0:T(8,128)(2,1)}), bf16[4,256,224]{1,2,0:T(8,128)(2,1)S(1)}, u32[]{:S(2)}, u32[]{:S(2)}) async-start(bf16[4,256,224]{1,2,0:T(8,128)(2,1)} %bitcast.129), calls=%async_computation | async-start | bytes 917504 | tf_op jit(solution)/shard_map/all_to_all | solution.py:503
  15.0 32.5 %copy-start.7 = (bf16[224,2432]{1,0:T(8,128)(2,1)S(1)}, bf16[224,2432]{1,0:T(8,128)(2,1)}, u32[]{:S(2)}) copy-start(bf16[224,2432]{1,0:T(8,128)(2,1)} %param.19) | copy-start | bytes 3268612
  15.0 142.3 %all-gather.7.cloned.1.call-start = ((), (), s32[]{:S(2)}) async-start(), calls=%async_computation.7 | async-start | bytes 2293760 | tf_op jit(solution)/shard_map/all_gather | solution.py:535
  55.5 18.0 %copy-start.38 = (f32[32]{0:T(128)}, f32[32]{0:T(128)S(1)}, u32[]{:S(2)}) copy-start(f32[32]{0:T(128)S(1)} %multiply_power_fusion) | copy-start | bytes 388
  66.8 40.2 %all-to-all-start.1 = ((bf16[4,224,640]{2,1,0:T(8,128)(2,1)}), bf16[4,224,640]{2,1,0:T(8,128)(2,1)S(1)}, u32[]{:S(2)}, u32[]{:S(2)}) async-start(bf16[4,224,640]{2,1,0:T(8,128)(2,1)} %pad_maximum_fusion), calls=%async_computation.1 | async-start | bytes 2293760 | tf_op jit(solution)/shard_map/all_to_all | solution.py:503
  70.9 31.7 %copy-start.29 = (f32[256]{0:T(256)}, f32[256]{0:T(256)S(1)}, u32[]{:S(2)}) copy-start(f32[256]{0:T(256)S(1)} %add_rsqrt_fusion.1) | copy-start | bytes 3076
  71.5 31.2 %copy-start.25 = (f32[4,1,224]{2,1,0:T(1,128)S(1)}, f32[4,1,224]{2,1,0:T(1,128)}, u32[]{:S(2)}) copy-start(f32[4,1,224]{2,1,0:T(1,128)} %get-tuple-element.99) | copy-start | bytes 10756
  73.5 28.6 %copy-start.15 = (f32[256,576]{0,1:T(8,128)}, f32[256,576]{0,1:T(8,128)S(1)}, u32[]{:S(2)}) copy-start(f32[256,576]{0,1:T(8,128)S(1)} %fusion.18) | copy-start | bytes 1769476
  74.4 32.7 %copy-start.18 = (f32[256,32]{0,1:T(8,128)}, f32[256,32]{0,1:T(8,128)S(1)}, u32[]{:S(2)}) copy-start(f32[256,32]{0,1:T(8,128)S(1)} %get-tuple-element.105) | copy-start | bytes 98308
  87.1 18.2 %collective-permute-start = (bf16[1024,128]{0,1:T(8,128)(2,1)}, bf16[1024,128]{0,1:T(8,128)(2,1)}, u32[]{:S(2)}, u32[]{:S(2)}) collective-permute-start(bf16[1024,128]{0,1:T(8,128)(2,1)} %all_gather.31), channel_id=1, source_target_pairs={{0,8},{8,16},{16,24},{24,32},{32,40},{40,48},{48,56},{56,64},{64,7... | collective-permute-start | bytes 786440 | tf_op jit(solution)/shard_map/ppermute | solution.py:32
  107.1 20.1 %all-to-all-start.3 = ((bf16[4,640,224]{1,2,0:T(8,128)(2,1)}), bf16[4,640,224]{1,2,0:T(8,128)(2,1)}, u32[]{:S(2)}, u32[]{:S(2)}) async-start(bf16[4,640,224]{1,2,0:T(8,128)(2,1)} %pad_maximum_fusion.2), calls=%async_computation.3 | async-start | bytes 2293760 | tf_op jit(solution)/shard_map/all_to_all | solution.py:503
  127.2 20.6 %all-to-all-start.2 = ((bf16[4,224,640]{2,1,0:T(8,128)(2,1)}), bf16[4,224,640]{2,1,0:T(8,128)(2,1)}, u32[]{:S(2)}, u32[]{:S(2)}) async-start(bf16[4,224,640]{2,1,0:T(8,128)(2,1)} %pad_maximum_fusion.1), calls=%async_computation.2 | async-start | bytes 2293760 | tf_op jit(solution)/shard_map/all_to_all | solution.py:503
  131.4 245.8 %reduce-scatter.2.cloned.1.call-start = ((), (), s32[]{:S(2)}) async-start(), calls=%async_computation.6 | async-start | bytes 327680 | tf_op jit(solution)/shard_map/reduce_scatter | solution.py:605
  137.6 10.2 %copy-start.39 = (pred[640]{0:T(1024)(128)(4,1)S(1)}, pred[640]{0:T(1024)(128)(4,1)}, u32[]{:S(2)}) copy-start(pred[640]{0:T(1024)(128)(4,1)} %fusion.54) | copy-start | bytes 1924
  139.6 15.1 %collective-permute-start.1 = (bf16[4,256,224]{2,1,0:T(8,128)(2,1)S(1)}, bf16[4,256,224]{2,1,0:T(8,128)(2,1)}, u32[]{:S(2)}, u32[]{:S(2)}) collective-permute-start(bf16[4,256,224]{2,1,0:T(8,128)(2,1)S(1)} %bitcast.141), channel_id=1, source_target_pairs={{0,1},{1,0},{2,3},{3,2},{4,5},{5,4},{6,7},{7,6},{8,9},{9,8},{10,11... | collective-permute-start | bytes 1376264 | tf_op jit(solution)/shard_map/ppermute | solution.py:444
  161.4 91.5 %copy-start.2 = (f32[4,256,224]{2,1,0:T(8,128)S(1)}, f32[4,256,224]{2,1,0:T(8,128)}, u32[]{:S(2)}) copy-start(f32[4,256,224]{2,1,0:T(8,128)} %copy-done.1) | copy-start | bytes 2752516
  161.4 91.5 %copy-start.28 = (f32[256]{0:T(256)S(1)}, f32[256]{0:T(256)}, u32[]{:S(2)}) copy-start(f32[256]{0:T(256)} %copy-done.27) | copy-start | bytes 3076
  161.4 93.7 %copy-start.37 = (f32[256]{0:T(256)S(1)}, f32[256]{0:T(256)}, u32[]{:S(2)}) copy-start(f32[256]{0:T(256)} %copy-done.36) | copy-start | bytes 3076
  257.0 9.1 %slice-start.2 = ((s8[9175040]{0:T(1024)(128)(4,1)}), s8[786432]{0:T(1024)(128)(4,1)S(1)}, s32[]{:S(2)}) async-start(s8[9175040]{0:T(1024)(128)(4,1)} %bitcast.132), calls=%async_computation.10 | async-start | bytes 1572864
  267.7 10.1 %copy-start.16 = (bf16[256,7,32]{0,2,1:T(8,128)(2,1)S(1)}, bf16[256,7,32]{0,2,1:T(8,128)(2,1)}, u32[]{:S(2)}) copy-start(bf16[256,7,32]{0,2,1:T(8,128)(2,1)} %get-tuple-element.93) | copy-start | bytes 344068
  267.7 10.1 %copy-start.17 = (bf16[256,7,32]{0,2,1:T(8,128)(2,1)S(1)}, bf16[256,7,32]{0,2,1:T(8,128)(2,1)}, u32[]{:S(2)}) copy-start(bf16[256,7,32]{0,2,1:T(8,128)(2,1)} %get-tuple-element.94) | copy-start | bytes 344068
  282.5 77.6 %collective-permute-start.2 = (bf16[1024,128]{0,1:T(8,128)(2,1)}, bf16[1024,128]{0,1:T(8,128)(2,1)}, u32[]{:S(2)}, u32[]{:S(2)}) collective-permute-start(bf16[1024,128]{0,1:T(8,128)(2,1)} %slice.237), channel_id=1, source_target_pairs={{8,0},{16,8},{24,16},{32,24},{40,32},{48,40},{56,48},{64,56},{72,6... | collective-permute-start | bytes 786440 | tf_op jit(solution)/shard_map/ppermute | solution.py:32
  361.9 16.3 %copy-start.33 = (f32[256]{0:T(256)S(1)}, f32[256]{0:T(256)}, u32[]{:S(2)}) copy-start(f32[256]{0:T(256)} %get-tuple-element.72) | copy-start | bytes 3076
  361.9 18.0 %copy-start.30 = (f32[256]{0:T(256)S(1)}, f32[256]{0:T(256)}, u32[]{:S(2)}) copy-start(f32[256]{0:T(256)} %copy-done.29) | copy-start | bytes 3076
  423.3 15.0 %collective-permute-start.3 = (bf16[4,256,224]{2,1,0:T(8,128)(2,1)S(1)}, bf16[4,256,224]{2,1,0:T(8,128)(2,1)S(1)}, u32[]{:S(2)}, u32[]{:S(2)}) collective-permute-start(bf16[4,256,224]{2,1,0:T(8,128)(2,1)S(1)} %bitcast.136), channel_id=1, source_target_pairs={{0,1},{1,0},{2,3},{3,2},{4,5},{5,4},{6,7},{7,6},{8,9},{9,8},{10,11... | collective-permute-start | bytes 1376264 | tf_op jit(solution)/shard_map/ppermute | solution.py:444
  427.3 11.6 %copy-start.35 = (f32[256]{0:T(256)S(1)}, f32[256]{0:T(256)}, u32[]{:S(2)}) copy-start(f32[256]{0:T(256)} %copy-done.34) | copy-start | bytes 3076
  427.3 11.6 %copy-start.31 = (f32[256]{0:T(256)S(1)}, f32[256]{0:T(256)}, u32[]{:S(2)}) copy-start(f32[256]{0:T(256)} %copy-done.29) | copy-start | bytes 3076
  440.2 278.8 %all-to-all-start.4 = ((bf16[4,256,224]{1,2,0:T(8,128)(2,1)}), bf16[4,256,224]{1,2,0:T(8,128)(2,1)S(1)}, u32[]{:S(2)}, u32[]{:S(2)}) async-start(bf16[4,256,224]{1,2,0:T(8,128)(2,1)} %copy.118), calls=%async_computation.5 | async-start | bytes 917504 | tf_op jit(solution)/shard_map/all_to_all | solution.py:503
  (26 other events, 96.6 us)
Sparse Core Ops, SparseCore 0:
  17.5 38.8 all-gather.6
  362.0 15.1 reduce-scatter.1
